TPU v7x, 32 devices: a whole 2x2x4 slice. The times are simulated.
32 devices in a mesh: ctx: 16 (over z, x, core), grp: 2 (over y).
Axes of the slice: x: 2, y: 2, z: 4, core: 2. Of those that a mesh axis runs over, the one named last changes fastest.
Arguments:
- query_in: bfloat16 [4096, 4096], P('grp', 'ctx'), may hold values from -6 to 6
- key_in: bfloat16 [4096, 4096], P('grp', 'ctx'), may hold values from -6 to 6
- value_in: bfloat16 [4096, 4096], P('grp', 'ctx'), may hold values from -6 to 6
- cotangent: bfloat16 [4096, 4096], P('grp', 'ctx'), may hold values from -6 to 6
- conv_filter: float32 [256, 4096], P(None, 'ctx'), may hold values from -0.9 to 0.9
Outputs:
- gated_out: bfloat16 [4096, 4096], P('grp', 'ctx')
- grad_query: bfloat16 [4096, 4096], P('grp', 'ctx')
- grad_key: bfloat16 [4096, 4096], P('grp', 'ctx')
- grad_value: bfloat16 [4096, 4096], P('grp', 'ctx')
- grad_filter: float32 [256, 4096], P(None, 'ctx')
All inputs are finite; a program needn't handle non-finite values.
Results may differ from a plain program's by a relative error of at most 0.0058.
Values may be sent and summed in bfloat16 or wider, within the bound.
A program may use at most 128 MiB of HBM per device.

v0:
```python
import functools
import math

import jax
import jax.numpy as jnp
from jax import lax
from jax.experimental import pallas as pl
from jax.experimental.pallas import tpu as pltpu
from jax.sharding import PartitionSpec as P

GROUP_CH = 16
HALF = 128
BF = jnp.bfloat16
F32 = jnp.float32


def build_toeplitz(taps_row, toep):
    seq = taps_row.shape[1]
    wide = jnp.broadcast_to(taps_row, (HALF, seq))
    rolled = pltpu.roll(wide, 0, 1, stride=1, stride_axis=0)
    row = lax.broadcasted_iota(jnp.int32, (HALF, HALF), 0)
    lane = lax.broadcasted_iota(jnp.int32, (HALF, HALF), 1)
    toep[:, :HALF] = jnp.zeros((HALF, HALF), BF)
    toep[:, HALF : 2 * HALF] = jnp.where(lane >= row, rolled[:, :HALF], 0.0).astype(BF)
    toep[:, 2 * HALF :] = rolled[:, HALF:].astype(BF)


def toeplitz_block(toep, lag, size):
    at = lag * size
    return jnp.concatenate(
        [toep[:, HALF + at : HALF + at + size], toep[:, at : at + size]], axis=0
    )


def group_step(n, size, x_ref, d_ref, f_ref, conv_ref, dmix_ref, part_ref, toep, dpad, acc, acc2):
    rows = n * GROUP_CH
    seq = n * size
    x = x_ref[...].reshape(rows, size)
    d = d_ref[...].reshape(rows, size)
    build_toeplitz(f_ref[0], toep)
    dpad[:rows] = d
    dpad[rows:] = jnp.zeros((rows, size), BF)
    xt = x.T
    pieces = []
    held = None
    for lag in range(n):
        prod = jnp.dot(
            xt, dpad[lag * GROUP_CH : lag * GROUP_CH + rows], preferred_element_type=F32
        )
        top, bottom = prod[:HALF], prod[HALF:]
        if held is not None:
            pieces.append(held + bottom[:, :HALF])
        pieces.append(top[:, :HALF] + bottom[:, HALF:])
        held = top[:, HALF:]
    pieces.append(held)
    pieces.append(jnp.zeros((HALF, HALF), F32))
    total = None
    for r in range(HALF // 8):
        line = jnp.concatenate([p[8 * r : 8 * r + 8] for p in pieces], axis=1)
        if r:
            line = pltpu.roll(line, seq + HALF - 8 * r, 1)
        total = line if total is None else total + line
    out = total[0:1, :]
    for s in range(1, 8):
        out = out + pltpu.roll(total, seq + HALF - s, 1)[s : s + 1, :]
    part_ref[0] = out[:, :seq]
    for lag in range(n):
        keep = rows - lag * GROUP_CH
        block = toeplitz_block(toep, lag, size)
        fwd = jnp.dot(x[:keep], block, preferred_element_type=F32)
        bwd = lax.dot_general(
            d[rows - keep :], block, (((1,), (1,)), ((), ())), preferred_element_type=F32
        )
        if lag == 0:
            acc[...] = fwd
            acc2[...] = bwd
        else:
            acc[rows - keep :] += fwd
            acc2[:keep] += bwd
    conv_ref[...] = acc[...].astype(BF).reshape(n, GROUP_CH, size)
    dmix_ref[...] = acc2[...].astype(BF).reshape(n, GROUP_CH, size)


def convolve(x, d, taps):
    n, width, size = x.shape
    groups = width // GROUP_CH
    rows = n * GROUP_CH
    seq = n * size
    wide_spec = pl.BlockSpec((n, GROUP_CH, size), lambda g: (0, g, 0))
    row_spec = pl.BlockSpec((1, 1, seq), lambda g: (g, 0, 0))
    return pl.pallas_call(
        functools.partial(group_step, n, size),
        grid=(groups,),
        out_shape=(
            jax.ShapeDtypeStruct(x.shape, BF),
            jax.ShapeDtypeStruct(x.shape, BF),
            jax.ShapeDtypeStruct((groups, 1, seq), F32),
        ),
        in_specs=[wide_spec, wide_spec, row_spec],
        out_specs=(wide_spec, wide_spec, row_spec),
        scratch_shapes=[
            pltpu.VMEM((HALF, HALF + seq), BF),
            pltpu.VMEM((2 * rows, size), BF),
            pltpu.VMEM((rows, size), F32),
            pltpu.VMEM((rows, size), F32),
        ],
        compiler_params=pltpu.CompilerParams(vmem_limit_bytes=40 * 1024 * 1024),
        cost_estimate=pl.CostEstimate(
            flops=6 * groups * rows * size * seq, bytes_accessed=8 * n * width * size, transcendentals=0
        ),
    )(x, d, taps)


def swap(blocks):
    return lax.all_to_all(blocks, "ctx", split_axis=0, concat_axis=0, tiled=True)


def per_device(query_in, key_in, value_in, cotangent, conv_filter):
    rows_grp, size = query_in.shape
    n = lax.axis_size("ctx")
    seq = size * n
    width = rows_grp // n
    groups = width // GROUP_CH
    group_dev = rows_grp // GROUP_CH
    blocks = (n, width, size)
    mine = lax.dynamic_slice_in_dim(conv_filter, lax.axis_index("grp") * group_dev, group_dev, 0)
    taps = swap(mine.reshape(n, groups, size))
    taps = jnp.transpose(taps, (1, 0, 2)).reshape(groups, 1, seq)
    q, k = query_in.astype(F32), key_in.astype(F32)
    v, c = value_in.astype(F32), cotangent.astype(F32)
    mixed = swap((k * v).astype(BF).reshape(blocks))
    dconv = swap((c * q).astype(BF).reshape(blocks))
    conv, dmixed, part = convolve(mixed, dconv, taps)
    conv = swap(conv).reshape(rows_grp, size).astype(F32)
    dmixed = swap(dmixed).reshape(rows_grp, size).astype(F32)
    part = swap(jnp.transpose(part.reshape(groups, n, size), (1, 0, 2))).reshape(group_dev, size)
    grad_filter = lax.all_gather(part, "grp", axis=0, tiled=True) / math.sqrt(GROUP_CH * seq)
    return (
        (q * conv).astype(BF),
        (c * conv).astype(BF),
        (dmixed * v).astype(BF),
        (dmixed * k).astype(BF),
        grad_filter,
    )


def solution(mesh):
    wide = P("grp", "ctx")
    return jax.shard_map(
        per_device,
        mesh=mesh,
        in_specs=(wide, wide, wide, wide, P(None, "ctx")),
        out_specs=(wide, wide, wide, wide, P(None, "ctx")),
        check_vma=False,
    )
```

profile of v0, /device:TPU:0, one launch (start us, length us, event | category | flops | bytes accessed | tf_op | source)
XLA Modules:
  0.0 164.4 jit_solution(14159034390526346021)
XLA Ops:
  0.6 0.0 copy-start
  0.7 0.9 copy-done
  1.6 0.7 dynamic-slice_bitcast_fusion
  2.3 7.4 %all-to-all-start.2 = ((f32[16,8,256]{2,1,0:T(8,128)}), f32[16,8,256]{2,1,0:T(8,128)S(1)}, u32[]{:S(2)}, u32[]{:S(2)}) async-start(f32[16,8,256]{2,1,0:T(8,128)} %dynamic-slice_bitcast_fusion), calls=%async_computation.2 | async-start | bytes 262144 | tf_op jit(solution)/shard_map/all_to_all | solution.py:115
  9.6 2.8 %fusion = bf16[2048,256]{1,0:T(8,128)(2,1)} fusion(bf16[2048,256]{1,0:T(8,128)(2,1)} %param.7, bf16[2048,256]{1,0:T(8,128)(2,1)} %param.6), kind=kLoop, calls=%fused_computation.6 | loop fusion | flops 2097152 | bytes 3145728 | tf_op jit(solution)/shard_map/convert_element_type | solution.py:131
  12.4 5.2 %all-to-all-done.2 = f32[16,8,256]{2,1,0:T(8,128)S(1)} async-done(((f32[16,8,256]{2,1,0:T(8,128)}), f32[16,8,256]{2,1,0:T(8,128)S(1)}, u32[]{:S(2)}, u32[]{:S(2)}) %all-to-all-start.2) | async-done | bytes 131104 | tf_op jit(solution)/shard_map/all_to_all | solution.py:115
  17.6 3.8 %all-to-all-start = ((bf16[16,128,256]{2,1,0:T(8,128)(2,1)}), bf16[16,128,256]{2,1,0:T(8,128)(2,1)S(1)}, u32[]{:S(2)}, u32[]{:S(2)}) async-start(bf16[16,128,256]{2,1,0:T(8,128)(2,1)} %bitcast.18), calls=%async_computation | async-start | bytes 2097152 | tf_op jit(solution)/shard_map/all_to_all | solution.py:115
  21.4 0.0 copy-done.4
  21.4 1.2 fusion.1
  22.6 21.6 %all-to-all-done.x_ref = bf16[16,128,256]{2,1,0:T(8,128)(2,1)S(1)} async-done(((bf16[16,128,256]{2,1,0:T(8,128)(2,1)}), bf16[16,128,256]{2,1,0:T(8,128)(2,1)S(1)}, u32[]{:S(2)}, u32[]{:S(2)}) %all-to-all-start) | async-done | bytes 1048608 | tf_op jit(solution)/shard_map/all_to_all | solution.py:115
  44.2 6.8 %all-to-all-start.1 = ((bf16[16,128,256]{2,1,0:T(8,128)(2,1)}), bf16[16,128,256]{2,1,0:T(8,128)(2,1)S(1)}, u32[]{:S(2)}, u32[]{:S(2)}) async-start(bf16[16,128,256]{2,1,0:T(8,128)(2,1)} %bitcast.17), calls=%async_computation.1 | async-start | bytes 2097152 | tf_op jit(solution)/shard_map/all_to_all | solution.py:115
  51.1 0.1 reshape.37.f_ref
  51.3 22.8 %all-to-all-done.1.d_ref = bf16[16,128,256]{2,1,0:T(8,128)(2,1)S(1)} async-done(((bf16[16,128,256]{2,1,0:T(8,128)(2,1)}), bf16[16,128,256]{2,1,0:T(8,128)(2,1)S(1)}, u32[]{:S(2)}, u32[]{:S(2)}) %all-to-all-start.1) | async-done | bytes 1048608 | tf_op jit(solution)/shard_map/all_to_all | solution.py:115
  74.0 14.4 %shard_map.92 = (bf16[16,128,256]{2,1,0:T(8,128)(2,1)}, bf16[16,128,256]{2,1,0:T(8,128)(2,1)S(1)}, f32[8,1,4096]{2,1,0:T(1,128)S(1)}) custom-call(bf16[16,128,256]{2,1,0:T(8,128)(2,1)S(1)} %all-to-all-done.x_ref, bf16[16,128,256]{2,1,0:T(8,128)(2,1)S(1)} %all-to-all-done.1.d_ref, f32[8,1,4096]{2,1,0:T(1,128)S(1)} %reshape.37.f_ref), custom_call_target="tpu_custom_call" | custom-call | flops 12884901888 | bytes 4194304 | tf_op jit(solution)/shard_map/pallas_call | solution.py:91
  88.4 0.7 copy-done.1
  89.1 1.2 reduce
  90.3 14.6 %all_to_all.30 = f32[16,8,256]{2,1,0:T(8,128)S(1)} all-to-all(f32[16,8,256]{2,1,0:T(8,128)S(1)} %bitcast.21), channel_id=1, replica_groups=mesh['ctx'=16,'grp'=2] {'ctx'}, dimensions={0} | all-to-all | bytes 262144 | tf_op jit(solution)/shard_map/all_to_all | solution.py:115
  104.9 28.1 %all_to_all.31 = bf16[16,128,256]{2,1,0:T(8,128)(2,1)} all-to-all(bf16[16,128,256]{2,1,0:T(8,128)(2,1)S(1)} %get-tuple-element.9), channel_id=1, replica_groups=mesh['ctx'=16,'grp'=2] {'ctx'}, dimensions={0} | all-to-all | bytes 2097152 | tf_op jit(solution)/shard_map/all_to_all | solution.py:115
  133.0 5.1 %all-to-all-start.3 = ((bf16[16,128,256]{2,1,0:T(8,128)(2,1)}), bf16[16,128,256]{2,1,0:T(8,128)(2,1)}, u32[]{:S(2)}, u32[]{:S(2)}) async-start(bf16[16,128,256]{2,1,0:T(8,128)(2,1)} %get-tuple-element.8), calls=%async_computation.3 | async-start | bytes 2097152 | tf_op jit(solution)/shard_map/all_to_all | solution.py:115
  138.1 6.4 %all_gather.3 = f32[256,256]{1,0:T(8,128)S(1)} all-gather(f32[128,256]{1,0:T(8,128)S(1)} %bitcast.19), channel_id=1, replica_groups=mesh['ctx'=16,'grp'=2] {'grp'}, dimensions={0}, use_global_device_ids=true | all-gather | bytes 393216 | tf_op jit(solution)/shard_map/all_gather | solution.py:137
  144.5 0.7 broadcast_multiply_fusion
  145.2 3.1 %fusion.5 = (bf16[2048,256]{1,0:T(8,128)(2,1)}, bf16[2048,256]{1,0:T(8,128)(2,1)}) fusion(bf16[2048,256]{1,0:T(8,128)(2,1)S(1)} %copy-done.3, bf16[16,128,256]{2,1,0:T(8,128)(2,1)} %all_to_all.31, bf16[2048,256]{1,0:T(8,128)(2,1)S(1)} %copy-done.2), kind=kLoop, calls=%fused_computation.11 | loop fusion | flops 3670016 | bytes 5242880 | tf_op jit(solution)/shard_map/convert_element_type | solution.py:142
  148.4 12.7 %all-to-all-done.3 = bf16[16,128,256]{2,1,0:T(8,128)(2,1)} async-done(((bf16[16,128,256]{2,1,0:T(8,128)(2,1)}), bf16[16,128,256]{2,1,0:T(8,128)(2,1)}, u32[]{:S(2)}, u32[]{:S(2)}) %all-to-all-start.3) | async-done | bytes 1048608 | tf_op jit(solution)/shard_map/all_to_all | solution.py:115
  161.1 3.4 %fusion.3 = (bf16[2048,256]{1,0:T(8,128)(2,1)}, bf16[2048,256]{1,0:T(8,128)(2,1)}) fusion(bf16[2048,256]{1,0:T(8,128)(2,1)S(1)} %copy-done.5, bf16[16,128,256]{2,1,0:T(8,128)(2,1)} %all-to-all-done.3, bf16[2048,256]{1,0:T(8,128)(2,1)} %param.5), kind=kLoop, calls=%fused_computation.9 | loop fusion | flops 3670016 | bytes 5242880 | tf_op jit(solution)/shard_map/convert_element_type | solution.py:140
  (11 shorter events, 0.1 us)
Async XLA Ops:
  0.6 1.0 copy-start
  2.3 15.3 %all-to-all-start.2 = ((f32[16,8,256]{2,1,0:T(8,128)}), f32[16,8,256]{2,1,0:T(8,128)S(1)}, u32[]{:S(2)}, u32[]{:S(2)}) async-start(f32[16,8,256]{2,1,0:T(8,128)} %dynamic-slice_bitcast_fusion), calls=%async_computation.2 | async-start | bytes 262144 | tf_op jit(solution)/shard_map/all_to_all | solution.py:115
  17.6 3.8 %copy-start.4 = (bf16[2048,256]{1,0:T(8,128)(2,1)S(1)}, bf16[2048,256]{1,0:T(8,128)(2,1)}, u32[]{:S(2)}) copy-start(bf16[2048,256]{1,0:T(8,128)(2,1)} %param.8) | copy-start | bytes 3145732
  17.6 3.8 %copy-start.6 = (bf16[2048,256]{1,0:T(8,128)(2,1)S(1)}, bf16[2048,256]{1,0:T(8,128)(2,1)}, u32[]{:S(2)}) copy-start(bf16[2048,256]{1,0:T(8,128)(2,1)} %param.5) | copy-start | bytes 3145732
  17.6 26.7 %all-to-all-start = ((bf16[16,128,256]{2,1,0:T(8,128)(2,1)}), bf16[16,128,256]{2,1,0:T(8,128)(2,1)S(1)}, u32[]{:S(2)}, u32[]{:S(2)}) async-start(bf16[16,128,256]{2,1,0:T(8,128)(2,1)} %bitcast.18), calls=%async_computation | async-start | bytes 2097152 | tf_op jit(solution)/shard_map/all_to_all | solution.py:115
  44.2 29.8 %all-to-all-start.1 = ((bf16[16,128,256]{2,1,0:T(8,128)(2,1)}), bf16[16,128,256]{2,1,0:T(8,128)(2,1)S(1)}, u32[]{:S(2)}, u32[]{:S(2)}) async-start(bf16[16,128,256]{2,1,0:T(8,128)(2,1)} %bitcast.17), calls=%async_computation.1 | async-start | bytes 2097152 | tf_op jit(solution)/shard_map/all_to_all | solution.py:115
  88.4 0.7 copy-start.1
  133.0 12.3 %copy-start.2 = (bf16[2048,256]{1,0:T(8,128)(2,1)S(1)}, bf16[2048,256]{1,0:T(8,128)(2,1)}, u32[]{:S(2)}) copy-start(bf16[2048,256]{1,0:T(8,128)(2,1)} %param.7) | copy-start | bytes 3145732
  133.0 12.3 %copy-start.3 = (bf16[2048,256]{1,0:T(8,128)(2,1)S(1)}, bf16[2048,256]{1,0:T(8,128)(2,1)}, u32[]{:S(2)}) copy-start(bf16[2048,256]{1,0:T(8,128)(2,1)} %param.6) | copy-start | bytes 3145732
  133.0 28.1 %all-to-all-start.3 = ((bf16[16,128,256]{2,1,0:T(8,128)(2,1)}), bf16[16,128,256]{2,1,0:T(8,128)(2,1)}, u32[]{:S(2)}, u32[]{:S(2)}) async-start(bf16[16,128,256]{2,1,0:T(8,128)(2,1)} %get-tuple-element.8), calls=%async_computation.3 | async-start | bytes 2097152 | tf_op jit(solution)/shard_map/all_to_all | solution.py:115
  145.2 15.8 %copy-start.5 = (bf16[2048,256]{1,0:T(8,128)(2,1)S(1)}, bf16[2048,256]{1,0:T(8,128)(2,1)}, u32[]{:S(2)}) copy-start(bf16[2048,256]{1,0:T(8,128)(2,1)} %param.8) | copy-start | bytes 3145732
where the time goes:
time: 166 us; the launch traced here: 164 us
  waiting for transfers between devices  62.3 us (38%)
  blocking collectives  49.1 us (30%)
  starting transfers between devices  23.1 us (14%)
  Pallas kernels  14.4 us (9%)
  other arithmetic  12.4 us (7%)
  local copies, waits for them, and re-layouts  2.46 us (1%)
    all_to_all x4, waiting for transfers between devices, swap(): lax.all_to_all(blocks, 'ctx', split_axis=0, concat_axis=0, tiled=True)  62.3 us
    all_to_all x2, blocking collectives, swap(): lax.all_to_all(blocks, 'ctx', split_axis=0, concat_axis=0, tiled=True)  42.7 us
    all_to_all x4, starting transfers between devices, swap(): lax.all_to_all(blocks, 'ctx', split_axis=0, concat_axis=0, tiled=True)  23.1 us
    pallas_call x1, Pallas kernels, convolve(): pl.pallas_call(functools.partial(group_step, n, size), grid=(groups,), ou...  14.4 us
    all_gather x1, blocking collectives, per_device(): lax.all_gather(part, 'grp', axis=0, tiled=True) / math.sqrt(GROUP_CH * seq)  6.42 us
    convert_element_type x1, other arithmetic, per_device(): (c * conv).astype(BF)  3.35 us
  transfers between devices with their start and end apart: 4, of which 4 were waited for; matrix products, arithmetic and copies ran while one was open for 5% of the time, Pallas kernels for 0%

commit v1 on v0

v1 whole, which is shorter than its diff:
```python
import functools
import math

import jax
import jax.numpy as jnp
from jax import lax
from jax.experimental import pallas as pl
from jax.experimental.pallas import tpu as pltpu
from jax.sharding import PartitionSpec as P

GROUP_CH = 16
HALF = 128
BF = jnp.bfloat16
F32 = jnp.float32
MESH = pl.DeviceIdType.MESH
CHUNKS = 4


def build_toeplitz(taps_row, toep):
    seq = taps_row.shape[1]
    wide = jnp.broadcast_to(taps_row, (HALF, seq))
    rolled = pltpu.roll(wide, 0, 1, stride=1, stride_axis=0)
    row = lax.broadcasted_iota(jnp.int32, (HALF, HALF), 0)
    lane = lax.broadcasted_iota(jnp.int32, (HALF, HALF), 1)
    toep[:, :HALF] = jnp.zeros((HALF, HALF), BF)
    toep[:, HALF : 2 * HALF] = jnp.where(lane >= row, rolled[:, :HALF], 0.0).astype(BF)
    toep[:, 2 * HALF :] = rolled[:, HALF:].astype(BF)


def toeplitz_block(toep, lag, size):
    at = lag * size
    return jnp.concatenate(
        [toep[:, HALF + at : HALF + at + size], toep[:, at : at + size]], axis=0
    )


def diagonal_sums(pieces, seq):
    total = None
    for r in range(HALF // 8):
        line = jnp.concatenate([p[8 * r : 8 * r + 8] for p in pieces], axis=1)
        if r:
            line = pltpu.roll(line, seq + HALF - 8 * r, 1)
        total = line if total is None else total + line
    out = total[0:1, :]
    for s in range(1, 8):
        out = out + pltpu.roll(total, seq + HALF - s, 1)[s : s + 1, :]
    return out[:, :seq]


def nn_dot(a, b):
    return jnp.dot(a, b, preferred_element_type=F32)


def nt_dot(a, b):
    return lax.dot_general(a, b, (((1,), (1,)), ((), ())), preferred_element_type=F32)


def kernel(
    n, grps, width, chunks, size,
    q_ref, k_ref, v_ref, c_ref, f_ref,
    gated_ref, gq_ref, gk_ref, gv_ref, gf_ref,
    mixed_st, dconv_st, xb, db, tapb, conv_st, dmix_st, conv_rc, dmix_rc,
    part_st, part_rc, filt_st, filt_rc, toep, dpad, acc, acc2,
    tap_s, tap_r, x_s, x_r, d_s, d_r, cv_s, cv_r, dm_s, dm_r, pt_s, pt_r, fl_s, fl_r,
):
    me = lax.axis_index("ctx")
    grp = lax.axis_index("grp")
    h = n // 2
    side, lane = me // h, lax.rem(me, h)
    cw = width // chunks
    gpc = cw // GROUP_CH
    rows = h * GROUP_CH
    seq = n * size

    barrier = pltpu.get_barrier_semaphore()

    @pl.loop(1, n)
    def _(r):
        pl.semaphore_signal(barrier, inc=1, device_id={"ctx": lax.rem(me + r, n)}, device_id_type=MESH)

    @pl.loop(1, grps)
    def _(r):
        pl.semaphore_signal(barrier, inc=1, device_id={"grp": lax.rem(grp + r, grps)}, device_id_type=MESH)

    def send(src, dst, ssem, rsem, to):
        pltpu.make_async_remote_copy(
            src_ref=src, dst_ref=dst, send_sem=ssem, recv_sem=rsem,
            device_id={"ctx": to}, device_id_type=MESH,
        ).start()

    def drain(ref, sem):
        pltpu.make_async_copy(ref, ref, sem).wait()

    def product(c):
        @pl.loop(0, h)
        def _(i):
            at = pl.ds(pl.multiple_of(i * width + c * cw, GROUP_CH), cw)
            mixed_st[at, :] = (k_ref[at, :].astype(F32) * v_ref[at, :].astype(F32)).astype(BF)
            dconv_st[at, :] = (c_ref[at, :].astype(F32) * q_ref[at, :].astype(F32)).astype(BF)

    def ship(c):
        def block(st, to):
            return st.at[pl.ds(pl.multiple_of(lax.rem(to, h) * width + c * cw, GROUP_CH), cw)]

        def to_other(st, buf, ssem, rsem):
            @pl.loop(0, h)
            def _(r):
                to = (1 - side) * h + lax.rem(lane + r, h)
                send(block(st, to), buf.at[c, me], ssem.at[c], rsem.at[c], to)

        @pl.when(side == 0)
        def _():
            to_other(mixed_st, xb, x_s, x_r)

        @pl.when(side == 1)
        def _():
            to_other(dconv_st, db, d_s, d_r)

        @pl.loop(1, h)
        def _(r):
            to = side * h + lax.rem(lane + r, h)
            send(block(mixed_st, to), xb.at[c, me], x_s.at[c], x_r.at[c], to)
            send(block(dconv_st, to), db.at[c, me], d_s.at[c], d_r.at[c], to)

        own = pl.ds(pl.multiple_of(lane * width + c * cw, GROUP_CH), cw)
        xb[c, me] = mixed_st[own, :]
        db[c, me] = dconv_st[own, :]

    product(0)
    pl.semaphore_wait(barrier, n - 1 + grps - 1)

    @pl.loop(1, n)
    def _(r):
        to = lax.rem(me + r, n)
        send(f_ref.at[lax.rem(to, h)], tapb.at[me], tap_s, tap_r, to)

    tapb[me] = f_ref[lane]
    ship(0)

    @pl.loop(1, chunks)
    def _(c):
        product(c)
        ship(c)

    drain(tapb.at[pl.ds(0, n - 1)], tap_r)

    def finish(c, few, few_sem, many, many_sem):
        drain(few.at[c, pl.ds(0, h - 1)], few_sem.at[c])
        drain(many.at[c, pl.ds(0, n - 1)], many_sem.at[c])

    def arrived(c):
        @pl.when(side == 0)
        def _():
            finish(c, xb, x_r, db, d_r)

        @pl.when(side == 1)
        def _():
            finish(c, db, d_r, xb, x_r)

    def departed(c):
        @pl.when(side == 0)
        def _():
            finish(c, db, d_s, xb, x_s)

        @pl.when(side == 1)
        def _():
            finish(c, xb, x_s, db, d_s)

    dpad[rows:] = jnp.zeros((2 * rows, size), BF)

    def group(c, g):
        at = pl.ds(pl.multiple_of(g * GROUP_CH, GROUP_CH), GROUP_CH)
        mine = pl.ds(side * h, h)
        x = xb[c, mine, at, :].reshape(rows, size)
        d = db[c, mine, at, :].reshape(rows, size)
        which = pl.ds(c * gpc + g, 1)
        build_toeplitz(jnp.concatenate([tapb[j, which, :] for j in range(n)], axis=1), toep)
        dpad[:rows] = d

        @pl.when(side == 0)
        def _():
            dpad[rows : 2 * rows] = db[c, h:, at, :].reshape(rows, size)

        xt = x.T
        pieces = []
        held = None
        for lag in range(n):
            prod = nn_dot(xt, dpad[lag * GROUP_CH : lag * GROUP_CH + rows])
            top, bottom = prod[:HALF], prod[HALF:]
            if held is not None:
                pieces.append(held + bottom[:, :HALF])
            pieces.append(top[:, :HALF] + bottom[:, HALF:])
            held = top[:, HALF:]
        pieces.append(held)
        pieces.append(jnp.zeros((HALF, HALF), F32))
        sums = diagonal_sums(pieces, seq)
        for j in range(n):
            part_st[c, j, pl.ds(g, 1), :] = sums[:, j * size : (j + 1) * size]
        for lag in range(h):
            keep = rows - lag * GROUP_CH
            block = toeplitz_block(toep, lag, size)
            fwd = nn_dot(x[:keep], block)
            bwd = nt_dot(d[rows - keep :], block)
            if lag == 0:
                acc[...] = fwd
                acc2[...] = bwd
            else:
                acc[rows - keep :] += fwd
                acc2[:keep] += bwd

        @pl.when(side == 1)
        def _():
            low = xb[c, :h, at, :].reshape(rows, size)
            for lag in range(1, n):
                block = toeplitz_block(toep, lag, size)
                cut = GROUP_CH * (lag if lag <= h else lag - h)
                if lag <= h:
                    acc[:cut] += nn_dot(low[rows - cut :], block)
                else:
                    acc[cut:] += nn_dot(low[: rows - cut], block)

        @pl.when(side == 0)
        def _():
            high = db[c, h:, at, :].reshape(rows, size)
            for lag in range(1, n):
                block = toeplitz_block(toep, lag, size)
                cut = GROUP_CH * (lag if lag <= h else lag - h)
                if lag <= h:
                    acc2[rows - cut :] += nt_dot(high[:cut], block)
                else:
                    acc2[: rows - cut] += nt_dot(high[cut:], block)

        conv_st[c, :, at, :] = acc[...].astype(BF).reshape(h, GROUP_CH, size)
        dmix_st[c, :, at, :] = acc2[...].astype(BF).reshape(h, GROUP_CH, size)

    @pl.loop(0, chunks)
    def _(c):
        arrived(c)

        @pl.loop(0, gpc)
        def _(g):
            group(c, g)

        own = pl.ds(pl.multiple_of(lane * width + c * cw, GROUP_CH), cw)

        @pl.loop(1, h)
        def _(r):
            i = lax.rem(lane + r, h)
            to = side * h + i
            send(conv_st.at[c, i], conv_rc.at[own], cv_s.at[c], cv_r.at[c], to)
            send(dmix_st.at[c, i], dmix_rc.at[own], dm_s.at[c], dm_r.at[c], to)

        @pl.loop(1, n)
        def _(r):
            to = lax.rem(me + r, n)
            send(part_st.at[c, to], part_rc.at[c, me], pt_s.at[c], pt_r.at[c], to)

        conv_rc[own, :] = conv_st[c, lane]
        dmix_rc[own, :] = dmix_st[c, lane]
        part_rc[c, me] = part_st[c, me]

    @pl.loop(0, chunks)
    def _(c):
        drain(conv_st.at[c, pl.ds(0, h - 1)], cv_r.at[c])
        drain(dmix_st.at[c, pl.ds(0, h - 1)], dm_r.at[c])

        @pl.loop(0, h)
        def _(i):
            at = pl.ds(pl.multiple_of(i * width + c * cw, GROUP_CH), cw)
            conv = conv_rc[at, :].astype(F32)
            dmixed = dmix_rc[at, :].astype(F32)
            gated_ref[at, :] = (q_ref[at, :].astype(F32) * conv).astype(BF)
            gq_ref[at, :] = (c_ref[at, :].astype(F32) * conv).astype(BF)
            gk_ref[at, :] = (dmixed * v_ref[at, :].astype(F32)).astype(BF)
            gv_ref[at, :] = (dmixed * k_ref[at, :].astype(F32)).astype(BF)

    scale = 1.0 / math.sqrt(GROUP_CH * seq)

    @pl.loop(0, chunks)
    def _(c):
        drain(part_st.at[c, pl.ds(0, n - 1)], pt_r.at[c])
        filt_st[c] = (part_rc[c, :h] + part_rc[c, h:]) * scale

    @pl.loop(1, grps)
    def _(r):
        pltpu.make_async_remote_copy(
            src_ref=filt_st, dst_ref=filt_rc.at[grp], send_sem=fl_s, recv_sem=fl_r,
            device_id={"grp": lax.rem(grp + r, grps)}, device_id_type=MESH,
        ).start()

    filt_rc[grp] = filt_st[...]

    drain(tapb.at[pl.ds(0, n - 1)], tap_s)

    @pl.loop(0, chunks)
    def _(c):
        departed(c)
        drain(conv_st.at[c, pl.ds(0, h - 1)], cv_s.at[c])
        drain(dmix_st.at[c, pl.ds(0, h - 1)], dm_s.at[c])
        drain(part_st.at[c, pl.ds(0, n - 1)], pt_s.at[c])

    drain(filt_rc.at[pl.ds(0, grps - 1)], fl_r)
    gf_ref[...] = filt_rc[...]
    drain(filt_rc.at[pl.ds(0, grps - 1)], fl_s)


def per_device(query_in, key_in, value_in, cotangent, conv_filter):
    rows_grp, size = query_in.shape
    n, grps = lax.axis_size("ctx"), lax.axis_size("grp")
    h = n // 2
    seq = size * n
    width = rows_grp // h
    groups = width // GROUP_CH
    chunks = min(CHUNKS, groups)
    cw = width // chunks
    gpc = groups // chunks
    group_dev = rows_grp // GROUP_CH
    mine = lax.dynamic_slice_in_dim(conv_filter, lax.axis_index("grp") * group_dev, group_dev, 0)
    rows = h * GROUP_CH
    wide = jax.ShapeDtypeStruct((rows_grp, size), BF)
    vmem = pl.BlockSpec(memory_space=pltpu.VMEM)
    dma = pltpu.SemaphoreType.DMA
    *outs, filt = pl.pallas_call(
        functools.partial(kernel, n, grps, width, chunks, size),
        out_shape=(wide, wide, wide, wide, jax.ShapeDtypeStruct((grps, chunks, h, gpc, size), F32)),
        in_specs=[vmem] * 5,
        out_specs=(vmem,) * 5,
        scratch_shapes=[
            pltpu.VMEM((rows_grp, size), BF),
            pltpu.VMEM((rows_grp, size), BF),
            pltpu.VMEM((chunks, n, cw, size), BF),
            pltpu.VMEM((chunks, n, cw, size), BF),
            pltpu.VMEM((n, groups, size), F32),
            pltpu.VMEM((chunks, h, cw, size), BF),
            pltpu.VMEM((chunks, h, cw, size), BF),
            pltpu.VMEM((rows_grp, size), BF),
            pltpu.VMEM((rows_grp, size), BF),
            pltpu.VMEM((chunks, n, gpc, size), F32),
            pltpu.VMEM((chunks, n, gpc, size), F32),
            pltpu.VMEM((chunks, h, gpc, size), F32),
            pltpu.VMEM((grps, chunks, h, gpc, size), F32),
            pltpu.VMEM((HALF, HALF + seq), BF),
            pltpu.VMEM((3 * rows, size), BF),
            pltpu.VMEM((rows, size), F32),
            pltpu.VMEM((rows, size), F32),
            dma, dma,
            dma((chunks,)), dma((chunks,)), dma((chunks,)), dma((chunks,)),
            dma((chunks,)), dma((chunks,)), dma((chunks,)), dma((chunks,)),
            dma((chunks,)), dma((chunks,)),
            dma, dma,
        ],
        compiler_params=pltpu.CompilerParams(
            collective_id=0, has_side_effects=True, vmem_limit_bytes=56 * 1024 * 1024
        ),
    )(query_in, key_in, value_in, cotangent, mine.reshape(h, groups, size))
    grad_filter = jnp.transpose(filt, (0, 2, 1, 3, 4)).reshape(grps * group_dev, size)
    return (*outs, grad_filter)


def solution(mesh):
    wide = P("grp", "ctx")
    return jax.shard_map(
        per_device,
        mesh=mesh,
        in_specs=(wide, wide, wide, wide, P(None, "ctx")),
        out_specs=(wide, wide, wide, wide, P(None, "ctx")),
        check_vma=False,
    )
```

time: 166 us -> 106 us (0.64)
  Pallas kernels: 14.4 us -> 95.3 us
  waiting for transfers between devices: 62.3 us -> 0 us
  blocking collectives: 49.1 us -> 0 us
  starting transfers between devices: 23.1 us -> 0 us
  other arithmetic: 12.4 us -> 0 us
  local copies, waits for them, and re-layouts: 2.46 us -> 9.24 us
    pallas_call x1, Pallas kernels: 14.4 us -> 95.3 us  [per_device(): pl.pallas_call(functools.partial(kernel, n, grps, width, chunks, size), o...]
    all_to_all x4 -> x0, waiting for transfers between devices: 62.3 us -> none  [swap(): lax.all_to_all(blocks, 'ctx', split_axis=0, concat_axis=0, tiled=True)]
    all_to_all x2 -> x0, blocking collectives: 42.7 us -> none  [swap(): lax.all_to_all(blocks, 'ctx', split_axis=0, concat_axis=0, tiled=True)]
    all_to_all x4 -> x0, starting transfers between devices: 23.1 us -> none  [swap(): lax.all_to_all(blocks, 'ctx', split_axis=0, concat_axis=0, tiled=True)]
    convert_element_type x4 -> x0, other arithmetic: 10.5 us -> none  [the longest x1 3.35 us: per_device(): (c * conv).astype(BF)]
    all_gather x1 -> x0, blocking collectives: 6.42 us -> none  [per_device(): lax.all_gather(part, 'grp', axis=0, tiled=True) / math.sqrt(GROUP_CH * seq)]
    unnamed x14, local copies, waits for them, and re-layouts: 1.62 us -> 6.72 us
  transfers between devices with their start and end apart: 4 -> 0, of which waited for: 4 -> 0; matrix products, arithmetic and copies ran while one was open for 5% -> 0% of each run, Pallas kernels for 0% -> 0%
where the time goes in v1:
time: 106 us; the launch traced here: 105 us
  Pallas kernels  95.3 us (90%)
  local copies, waits for them, and re-layouts  9.24 us (9%)
    pallas_call x1, Pallas kernels, per_device(): pl.pallas_call(functools.partial(kernel, n, grps, width, chunks, size), o...  95.3 us
    unnamed x14, local copies, waits for them, and re-layouts  6.72 us

profile of v1, /device:TPU:0, one launch (start us, length us, event | category | flops | bytes accessed | tf_op | source)
XLA Modules:
  0.0 105.2 jit_solution(10322407524243487210)
XLA Ops:
  0.6 0.0 copy-start
  0.7 0.9 copy-done
  1.6 0.7 constant_dynamic-slice_fusion
  2.3 95.3 %shard_map.92 = (bf16[2048,256]{1,0:T(8,128)(2,1)}, bf16[2048,256]{1,0:T(8,128)(2,1)}, bf16[2048,256]{1,0:T(8,128)(2,1)}, bf16[2048,256]{1,0:T(8,128)(2,1)}, f32[2,4,8,4,256]{4,3,2,1,0:T(4,128)}) custom-call(bf16[2048,256]{1,0:T(8,128)(2,1)} %q_ref.1, bf16[2048,256]{1,0:T(8,128)(2,1)} %k_ref.1, bf16[2048,256]{1,0:T(8,128)(2,1)} %v_ref.1, ...), custom_call_target="tpu_custom_call" | custom-call | tf_op jit(solution)/shard_map/pallas_call | solution.py:323
  97.6 0.0 copy-start.4
  97.6 1.1 %copy.10 = f32[2,8,4,4,256]{4,3,2,1,0:T(4,128)S(1)} copy(f32[2,8,4,4,256]{4,3,1,2,0:T(4,128)} %bitcast.3) | data formatting | bytes 524288 | tf_op jit(solution)/shard_map/transpose | solution.py:356
  98.7 0.8 reshape.17
  99.5 0.0 copy-done.4
  99.5 0.0 copy-start.3
  99.5 1.0 copy.15
  100.4 0.6 copy-done.3
  101.1 0.0 copy-start.2
  101.1 1.0 copy.16
  102.0 0.6 copy-done.2
  102.7 0.0 copy-start.1
  102.7 1.0 copy.17
  103.6 0.6 copy-done.1
  104.3 1.0 copy.18
Async XLA Ops:
  0.6 1.0 copy-start
  97.6 1.9 %copy-start.4 = (bf16[2048,256]{1,0:T(8,128)(2,1)S(1)}, bf16[2048,256]{1,0:T(8,128)(2,1)}, u32[]{:S(2)}) copy-start(bf16[2048,256]{1,0:T(8,128)(2,1)} %get-tuple-element.20) | copy-start | bytes 3145732
  99.5 1.6 %copy-start.3 = (bf16[2048,256]{1,0:T(8,128)(2,1)S(1)}, bf16[2048,256]{1,0:T(8,128)(2,1)}, u32[]{:S(2)}) copy-start(bf16[2048,256]{1,0:T(8,128)(2,1)} %get-tuple-element.21) | copy-start | bytes 3145732
  101.1 1.6 %copy-start.2 = (bf16[2048,256]{1,0:T(8,128)(2,1)S(1)}, bf16[2048,256]{1,0:T(8,128)(2,1)}, u32[]{:S(2)}) copy-start(bf16[2048,256]{1,0:T(8,128)(2,1)} %get-tuple-element.22) | copy-start | bytes 3145732
  102.7 1.6 %copy-start.1 = (bf16[2048,256]{1,0:T(8,128)(2,1)S(1)}, bf16[2048,256]{1,0:T(8,128)(2,1)}, u32[]{:S(2)}) copy-start(bf16[2048,256]{1,0:T(8,128)(2,1)} %get-tuple-element.23) | copy-start | bytes 3145732

commit v2 on v1

--- a/solution.py
+++ b/solution.py
@@ -58,7 +58,7 @@
 def kernel(
     n, grps, width, chunks, size,
     q_ref, k_ref, v_ref, c_ref, f_ref,
-    gated_ref, gq_ref, gk_ref, gv_ref, gf_ref,
+    conv_ref, dmix_ref, gf_ref,
     mixed_st, dconv_st, xb, db, tapb, conv_st, dmix_st, conv_rc, dmix_rc,
     part_st, part_rc, filt_st, filt_rc, toep, dpad, acc, acc2,
     tap_s, tap_r, x_s, x_r, d_s, d_r, cv_s, cv_r, dm_s, dm_r, pt_s, pt_r, fl_s, fl_r,
@@ -102,25 +102,29 @@
         def block(st, to):
             return st.at[pl.ds(pl.multiple_of(lax.rem(to, h) * width + c * cw, GROUP_CH), cw)]
 
-        def to_other(st, buf, ssem, rsem):
-            @pl.loop(0, h)
-            def _(r):
-                to = (1 - side) * h + lax.rem(lane + r, h)
-                send(block(st, to), buf.at[c, me], ssem.at[c], rsem.at[c], to)
-
-        @pl.when(side == 0)
-        def _():
-            to_other(mixed_st, xb, x_s, x_r)
-
-        @pl.when(side == 1)
-        def _():
-            to_other(dconv_st, db, d_s, d_r)
-
-        @pl.loop(1, h)
+        @pl.loop(0, h)
         def _(r):
-            to = side * h + lax.rem(lane + r, h)
-            send(block(mixed_st, to), xb.at[c, me], x_s.at[c], x_r.at[c], to)
-            send(block(dconv_st, to), db.at[c, me], d_s.at[c], d_r.at[c], to)
+            near = lax.rem(lane + r, h)
+            apart = lax.rem(lane + r + h // 2, h)
+            over = (1 - side) * h + near
+
+            @pl.when(side == 0)
+            def _():
+                send(block(mixed_st, over), xb.at[c, me], x_s.at[c], x_r.at[c], over)
+
+            @pl.when(side == 1)
+            def _():
+                send(block(dconv_st, over), db.at[c, me], d_s.at[c], d_r.at[c], over)
+
+            @pl.when(r != h // 2)
+            def _():
+                to = side * h + apart
+                send(block(mixed_st, to), xb.at[c, me], x_s.at[c], x_r.at[c], to)
+
+            @pl.when(r != 0)
+            def _():
+                to = side * h + near
+                send(block(dconv_st, to), db.at[c, me], d_s.at[c], d_r.at[c], to)
 
         own = pl.ds(pl.multiple_of(lane * width + c * cw, GROUP_CH), cw)
         xb[c, me] = mixed_st[own, :]
@@ -132,9 +136,9 @@
     @pl.loop(1, n)
     def _(r):
         to = lax.rem(me + r, n)
-        send(f_ref.at[lax.rem(to, h)], tapb.at[me], tap_s, tap_r, to)
-
-    tapb[me] = f_ref[lane]
+        send(f_ref.at[grp, lax.rem(to, h)], tapb.at[me], tap_s, tap_r, to)
+
+    tapb[me] = f_ref[grp, lane]
     ship(0)
 
     @pl.loop(1, chunks)
@@ -243,12 +247,18 @@
 
         own = pl.ds(pl.multiple_of(lane * width + c * cw, GROUP_CH), cw)
 
-        @pl.loop(1, h)
+        @pl.loop(0, h)
         def _(r):
-            i = lax.rem(lane + r, h)
-            to = side * h + i
-            send(conv_st.at[c, i], conv_rc.at[own], cv_s.at[c], cv_r.at[c], to)
-            send(dmix_st.at[c, i], dmix_rc.at[own], dm_s.at[c], dm_r.at[c], to)
+            near = lax.rem(lane + r, h)
+            apart = lax.rem(lane + r + h // 2, h)
+
+            @pl.when(r != h // 2)
+            def _():
+                send(conv_st.at[c, apart], conv_rc.at[own], cv_s.at[c], cv_r.at[c], side * h + apart)
+
+            @pl.when(r != 0)
+            def _():
+                send(dmix_st.at[c, near], dmix_rc.at[own], dm_s.at[c], dm_r.at[c], side * h + near)
 
         @pl.loop(1, n)
         def _(r):
@@ -267,12 +277,8 @@
         @pl.loop(0, h)
         def _(i):
             at = pl.ds(pl.multiple_of(i * width + c * cw, GROUP_CH), cw)
-            conv = conv_rc[at, :].astype(F32)
-            dmixed = dmix_rc[at, :].astype(F32)
-            gated_ref[at, :] = (q_ref[at, :].astype(F32) * conv).astype(BF)
-            gq_ref[at, :] = (c_ref[at, :].astype(F32) * conv).astype(BF)
-            gk_ref[at, :] = (dmixed * v_ref[at, :].astype(F32)).astype(BF)
-            gv_ref[at, :] = (dmixed * k_ref[at, :].astype(F32)).astype(BF)
+            conv_ref[at, :] = conv_rc[at, :]
+            dmix_ref[at, :] = dmix_rc[at, :]
 
     scale = 1.0 / math.sqrt(GROUP_CH * seq)
 
@@ -302,6 +308,28 @@
     drain(filt_rc.at[pl.ds(0, grps - 1)], fl_r)
     gf_ref[...] = filt_rc[...]
     drain(filt_rc.at[pl.ds(0, grps - 1)], fl_s)
+
+
+def steps_of(rows):
+    return max(1, rows // 512)
+
+
+def gate_step(q_ref, k_ref, v_ref, c_ref, conv_ref, dmix_ref, filt_ref,
+              gated_ref, gq_ref, gk_ref, gv_ref, gf_ref):
+    conv, dmixed = conv_ref[...].astype(F32), dmix_ref[...].astype(F32)
+    gated_ref[...] = (q_ref[...].astype(F32) * conv).astype(BF)
+    gq_ref[...] = (c_ref[...].astype(F32) * conv).astype(BF)
+    gk_ref[...] = (dmixed * v_ref[...].astype(F32)).astype(BF)
+    gv_ref[...] = (dmixed * k_ref[...].astype(F32)).astype(BF)
+
+    @pl.when(pl.program_id(0) == 0)
+    def _():
+        grps, chunks, h, gpc, _ = filt_ref.shape
+        for y in range(grps):
+            for i in range(h):
+                for c in range(chunks):
+                    at = ((y * h + i) * chunks + c) * gpc
+                    gf_ref[at : at + gpc] = filt_ref[y, c, i]
 
 
 def per_device(query_in, key_in, value_in, cotangent, conv_filter):
@@ -315,16 +343,15 @@
     cw = width // chunks
     gpc = groups // chunks
     group_dev = rows_grp // GROUP_CH
-    mine = lax.dynamic_slice_in_dim(conv_filter, lax.axis_index("grp") * group_dev, group_dev, 0)
     rows = h * GROUP_CH
     wide = jax.ShapeDtypeStruct((rows_grp, size), BF)
     vmem = pl.BlockSpec(memory_space=pltpu.VMEM)
     dma = pltpu.SemaphoreType.DMA
-    *outs, filt = pl.pallas_call(
+    conv, dmixed, filt = pl.pallas_call(
         functools.partial(kernel, n, grps, width, chunks, size),
-        out_shape=(wide, wide, wide, wide, jax.ShapeDtypeStruct((grps, chunks, h, gpc, size), F32)),
+        out_shape=(wide, wide, jax.ShapeDtypeStruct((grps, chunks, h, gpc, size), F32)),
         in_specs=[vmem] * 5,
-        out_specs=(vmem,) * 5,
+        out_specs=(vmem,) * 3,
         scratch_shapes=[
             pltpu.VMEM((rows_grp, size), BF),
             pltpu.VMEM((rows_grp, size), BF),
@@ -352,9 +379,18 @@
         compiler_params=pltpu.CompilerParams(
             collective_id=0, has_side_effects=True, vmem_limit_bytes=56 * 1024 * 1024
         ),
-    )(query_in, key_in, value_in, cotangent, mine.reshape(h, groups, size))
-    grad_filter = jnp.transpose(filt, (0, 2, 1, 3, 4)).reshape(grps * group_dev, size)
-    return (*outs, grad_filter)
+    )(query_in, key_in, value_in, cotangent, conv_filter.reshape(grps, h, groups, size))
+    tall = rows_grp // steps_of(rows_grp)
+    part_spec = pl.BlockSpec((tall, size), lambda i: (i, 0))
+    return pl.pallas_call(
+        gate_step,
+        grid=(steps_of(rows_grp),),
+        out_shape=(wide, wide, wide, wide, jax.ShapeDtypeStruct((grps * group_dev, size), F32)),
+        in_specs=[part_spec] * 6 + [pl.BlockSpec(filt.shape, lambda i: (0,) * 5)],
+        out_specs=(part_spec,) * 4
+        + (pl.BlockSpec((grps * group_dev, size), lambda i: (0, 0)),),
+        compiler_params=pltpu.CompilerParams(vmem_limit_bytes=32 * 1024 * 1024),
+    )(query_in, key_in, value_in, cotangent, conv, dmixed, filt)
 
 
 def solution(mesh):

time: 106 us -> 99.9 us (0.942)
  local copies, waits for them, and re-layouts: 9.24 us -> 3.41 us
    unnamed x14, local copies, waits for them, and re-layouts: 6.72 us -> 3.41 us
    pallas_call x0 -> x1, Pallas kernels: none -> 2.87 us  [per_device(): pl.pallas_call(gate_step, grid=(steps_of(rows_grp),), out_shape=(wide, wi...]
    pallas_call x1, Pallas kernels: 95.3 us -> 92.7 us  [per_device(): pl.pallas_call(functools.partial(kernel, n, grps, width, chunks, size), o...]
where the time goes in v2:
time: 99.9 us; the launch traced here: 99.7 us
  Pallas kernels  95.6 us (96%)
  local copies, waits for them, and re-layouts  3.41 us (3%)
    pallas_call x1, Pallas kernels, per_device(): pl.pallas_call(functools.partial(kernel, n, grps, width, chunks, size), o...  92.7 us
    unnamed x14, local copies, waits for them, and re-layouts  3.41 us
    pallas_call x1, Pallas kernels, per_device(): pl.pallas_call(gate_step, grid=(steps_of(rows_grp),), out_shape=(wide, wi...  2.87 us

profile of v2, /device:TPU:0, one launch (start us, length us, event | category | flops | bytes accessed | tf_op | source)
XLA Modules:
  0.0 99.7 jit_solution(2638541818479981640)
XLA Ops:
  0.6 0.0 copy-start
  0.6 0.0 copy-start.1
  0.7 0.0 copy-start.2
  0.7 0.0 copy-start.3
  0.7 92.7 %shard_map.92 = (bf16[2048,256]{1,0:T(8,128)(2,1)}, bf16[2048,256]{1,0:T(8,128)(2,1)}, f32[2,4,8,4,256]{4,3,2,1,0:T(4,128)}) custom-call(bf16[2048,256]{1,0:T(8,128)(2,1)} %q_ref.3, bf16[2048,256]{1,0:T(8,128)(2,1)} %k_ref.3, bf16[2048,256]{1,0:T(8,128)(2,1)} %v_ref.3, bf16[2048,256]{1,0:T(8,128)(2,1)} %c_ref.3, f32[2,8,16,256]{3,2,1,0:T(8,128)} %bitcast.1), custom_call_target="tpu_custom_call" | custom-call | tf_op jit(solution)/shard_map/pallas_call | solution.py:350
  93.4 0.0 copy-done
  93.4 0.0 copy-done.1
  93.4 0.0 copy-done.2
  93.4 0.0 copy-done.3
  93.4 0.0 copy-start.4
  93.4 1.2 %copy-done.4 = bf16[2048,256]{1,0:T(8,128)(2,1)S(1)} copy-done((bf16[2048,256]{1,0:T(8,128)(2,1)S(1)}, bf16[2048,256]{1,0:T(8,128)(2,1)}, u32[]{:S(2)}) %copy-start.4) | copy-done | bytes 1048600
  94.6 0.0 copy-start.5
  94.6 1.2 %copy-done.5 = bf16[2048,256]{1,0:T(8,128)(2,1)S(1)} copy-done((bf16[2048,256]{1,0:T(8,128)(2,1)S(1)}, bf16[2048,256]{1,0:T(8,128)(2,1)}, u32[]{:S(2)}) %copy-start.5) | copy-done | bytes 1048600
  95.9 0.0 copy-start.6
  95.9 0.9 copy-done.6
  96.8 2.9 %shard_map.93 = (bf16[2048,256]{1,0:T(8,128)(2,1)}, bf16[2048,256]{1,0:T(8,128)(2,1)}, bf16[2048,256]{1,0:T(8,128)(2,1)}, bf16[2048,256]{1,0:T(8,128)(2,1)}, f32[256,256]{1,0:T(8,128)}) custom-call(bf16[2048,256]{1,0:T(8,128)(2,1)S(1)} %copy-done, bf16[2048,256]{1,0:T(8,128)(2,1)S(1)} %copy-done.1, bf16[2048,256]{1,0:T(8,128)(2,1)S(1)} %copy-done.2, ...), custom_call_target="tpu_custom_call" | custom-call | tf_op jit(solution)/shard_map/pallas_call | solution.py:385
Async XLA Ops:
  0.6 92.7 %copy-start = (bf16[2048,256]{1,0:T(8,128)(2,1)S(1)}, bf16[2048,256]{1,0:T(8,128)(2,1)}, u32[]{:S(2)}) copy-start(bf16[2048,256]{1,0:T(8,128)(2,1)} %q_ref.3) | copy-start | bytes 3145732
  0.6 92.7 %copy-start.1 = (bf16[2048,256]{1,0:T(8,128)(2,1)S(1)}, bf16[2048,256]{1,0:T(8,128)(2,1)}, u32[]{:S(2)}) copy-start(bf16[2048,256]{1,0:T(8,128)(2,1)} %k_ref.3) | copy-start | bytes 3145732
  0.7 92.7 %copy-start.2 = (bf16[2048,256]{1,0:T(8,128)(2,1)S(1)}, bf16[2048,256]{1,0:T(8,128)(2,1)}, u32[]{:S(2)}) copy-start(bf16[2048,256]{1,0:T(8,128)(2,1)} %v_ref.3) | copy-start | bytes 3145732
  0.7 92.7 %copy-start.3 = (bf16[2048,256]{1,0:T(8,128)(2,1)S(1)}, bf16[2048,256]{1,0:T(8,128)(2,1)}, u32[]{:S(2)}) copy-start(bf16[2048,256]{1,0:T(8,128)(2,1)} %c_ref.3) | copy-start | bytes 3145732
  93.4 1.2 %copy-start.4 = (bf16[2048,256]{1,0:T(8,128)(2,1)S(1)}, bf16[2048,256]{1,0:T(8,128)(2,1)}, u32[]{:S(2)}) copy-start(bf16[2048,256]{1,0:T(8,128)(2,1)} %get-tuple-element.8.conv_ref) | copy-start | bytes 3145732
  94.6 1.2 %copy-start.5 = (bf16[2048,256]{1,0:T(8,128)(2,1)S(1)}, bf16[2048,256]{1,0:T(8,128)(2,1)}, u32[]{:S(2)}) copy-start(bf16[2048,256]{1,0:T(8,128)(2,1)} %get-tuple-element.9.dmix_ref) | copy-start | bytes 3145732
  95.9 0.9 copy-start.6
